TPU v7x, 256 devices: a whole 4x4x8 slice. The times are simulated.
256 devices in a mesh: dp: 4 (over y), space: 32 (over x_lo, z, core), tensor: 2 (over x_hi).
Axes of the slice: x: 4 (x_hi: 2, x_lo: 2; x = x_hi * 2 + x_lo), y: 4, z: 8, core: 2. Of those that a mesh axis runs over, the one named last changes fastest.
Arguments:
- queries: bfloat16 [4, 16, 256, 5120], P('dp', None, 'space', 'tensor'), may hold values from -60 to 60, as said below
- keys: bfloat16 [4, 16, 256, 5120], P('dp', None, 'space', 'tensor'), may hold values from -4 to 4
- values: bfloat16 [4, 16, 256, 5120], P('dp', None, 'space', 'tensor'), may hold values from -6 to 6
- cotangent: bfloat16 [4, 16, 256, 5120], P('dp', None, 'space', 'tensor'), may hold values from -6 to 6
- land: int32 [16, 256], replicated, may hold values 0 or 1
- shifts: int32 [2], replicated, may hold values from 1 to 7
- bias_network_first_weight: float32 [2, 512], replicated, may hold values from -4 to 4
- bias_network_first_offset: float32 [512], replicated, may hold values from -3 to 3
- bias_network_second_weight: float32 [512, 40], P(None, 'tensor'), may hold values from -0.25 to 0.25
- surface_key_bias: float32 [2, 40], P(None, 'tensor'), may hold values from -4 to 4
Outputs:
- grad_queries: bfloat16 [4, 16, 256, 5120], P('dp', None, 'space', 'tensor')
- grad_keys: bfloat16 [4, 16, 256, 5120], P('dp', None, 'space', 'tensor')
- grad_values: bfloat16 [4, 16, 256, 5120], P('dp', None, 'space', 'tensor')
- grad_first: float32 [2, 512], replicated
- grad_first_bias: float32 [512], replicated
- grad_second: float32 [512, 40], P(None, 'tensor')
- grad_key_bias: float32 [2, 40], P(None, 'tensor')
Inputs may be any that keep to these rules, and one draw needn't show every extreme that they name: queries: in the hidden draw some queries are aligned with their own key. shifts[0] is the latitude offset, shifts[1] the longitude offset.
All inputs are finite; a program needn't handle non-finite values.
Results may differ from a plain program's by a relative error of at most 0.02.
Values may be sent and summed in bfloat16 or wider, within the bound.
A program may use at most 128 MiB of HBM per device.

v0:
```python
import jax
import jax.numpy as jnp
from jax import lax
from jax.experimental import pallas as pl
from jax.experimental.pallas import tpu as pltpu
from jax.sharding import PartitionSpec as P

MESH = pl.DeviceIdType.MESH
MASKED = -1000000000.0
LOG2E = 1.4426950408889634
HEADS = 20
HALF = HEADS // 2
PAIR = 2
CHUNKS = HALF // PAIR
LANES = PAIR * 128
EAST = HALF * 128
BF16 = jnp.bfloat16
F32 = jnp.float32
HIGHEST = lax.Precision.HIGHEST


def iota(shape, dim):
    return lax.broadcasted_iota(jnp.int32, shape, dim)


def onehot(cond):
    return jnp.where(cond, 1.0, 0.0).astype(BF16)


def dot(a, b, ca, cb, precision=None):
    return lax.dot_general(
        a, b, (((ca,), (cb,)), ((), ())), preferred_element_type=F32, precision=precision
    )


def squash(t):
    t = t.astype(F32)
    size = jnp.log2(1.0 + jnp.abs(t)) / 3.0
    return jnp.where(t < 0, -size, size)


def hidden_before(first, offset):
    n = iota((256, 1), 0)
    dy, dx = n // 16, n % 16
    cy = squash(jnp.where(dy >= 8, dy - 16, dy))
    cx = squash(jnp.where(dx >= 8, dx - 16, dx))
    return cy * first[0:1, :] + cx * first[1:2, :] + offset, cy, cx


def used_bins(rows):
    n = iota((rows, 256), 1)
    return (n // 16 != 8) & (n % 16 != 8)


def three_parts(x):
    a = x.astype(BF16)
    rest = x - a.astype(F32)
    b = rest.astype(BF16)
    c = (rest - b.astype(F32)).astype(BF16)
    return jnp.concatenate([a, b, c], axis=0)


def main_kernel(
    q_ref,
    k_ref,
    v_ref,
    d_ref,
    land_hbm,
    shifts_hbm,
    first_hbm,
    offset_hbm,
    second_hbm,
    keybias_hbm,
    out_ref,
    sums_ref,
    seconds_ref,
    layer_ref,
    held,
    far,
    arrived,
    bias,
    expand,
    rows,
    land_rows,
    is_land,
    gather,
    place,
    table_part,
    near_part,
    z_part,
    land_ref,
    second_ref,
    shifts_ref,
    keybias_ref,
    load_sem,
    small_sem,
    in_send,
    in_recv,
    back_send,
    back_recv,
    second_sem,
    near_send,
    near_recv,
    z_send,
    z_recv,
    xy_send,
    xy_recv,
):
    y = lax.axis_index("dp")
    sp = lax.axis_index("space")
    t = lax.axis_index("tensor")
    core, z, x_lo = sp % 2, (sp // 2) % 8, sp // 16
    x = t * 2 + x_lo
    west_id = {"space": (sp + 31) % 32}
    east_id = {"space": (sp + 1) % 32}
    slow_id = {"space": (sp + 31 + 2 * core) % 32}
    near = []
    for k in range(1, 16):
        xx, yy, cc = (x_lo + k // 8) % 2, (y + (k // 2) % 4) % 4, (core + k) % 2
        near.append((xx * 4 + yy, {"dp": yy, "space": xx * 16 + z * 2 + cc}))
    z_ids = [{"space": x_lo * 16 + ((z + k) % 8) * 2 + core} for k in range(1, 8)]
    xy_ids = []
    for k in range(1, 16):
        xx, yy = (x + k // 4) % 4, (y + k % 4) % 4
        xy_ids.append({"dp": yy, "space": (xx % 2) * 16 + z * 2 + core, "tensor": xx // 2})
    other_ids = []
    for k in range(8):
        xx, yy = (x_lo + k // 4) % 2, (y + k % 4) % 4
        other_ids.append({"dp": yy, "space": xx * 16 + z * 2 + core, "tensor": 1 - t})
    tensor_id = {"tensor": 1 - t}

    barrier = pltpu.get_barrier_semaphore()
    for to in [slow_id] + [i for _, i in near] + z_ids + other_ids:
        pl.semaphore_signal(barrier, inc=1, device_id=to, device_id_type=MESH)

    fields = (q_ref, k_ref, v_ref, d_ref)
    small = [
        pltpu.make_async_copy(a, b, small_sem.at[i])
        for i, (a, b) in enumerate(
            (
                (shifts_hbm, shifts_ref),
                (land_hbm, land_ref),
                (first_hbm, layer_ref.at[pl.ds(0, 2)]),
                (offset_hbm, layer_ref.at[pl.ds(2, 1)]),
                (second_hbm, second_ref),
                (keybias_hbm, keybias_ref),
            )
        )
    ]
    for copy in small:
        copy.start()

    def lanes_of(side, c):
        return pl.ds(pl.multiple_of(side * EAST + c * LANES, LANES), LANES)

    def in_copy(side, a, c):
        lanes = lanes_of(side, c)
        return pltpu.make_async_remote_copy(
            src_ref=fields[a].at[:, :, lanes],
            dst_ref=held.at[a, pl.ds(16 - 16 * side, 16), :, lanes],
            send_sem=in_send.at[side, a, c],
            recv_sem=in_recv.at[side, a, c],
            device_id=east_id if side else west_id,
            device_id_type=MESH,
        )

    def back_copy(side, c):
        lanes = lanes_of(side, c)
        return pltpu.make_async_remote_copy(
            src_ref=far.at[:, :, :, lanes],
            dst_ref=arrived.at[:, :, :, lanes],
            send_sem=back_send.at[side, c],
            recv_sem=back_recv.at[side, c],
            device_id=west_id if side else east_id,
            device_id_type=MESH,
        )

    second_copy = pltpu.make_async_remote_copy(
        src_ref=second_hbm,
        dst_ref=seconds_ref.at[t],
        send_sem=second_sem.at[0],
        recv_sem=second_sem.at[1],
        device_id=tensor_id,
        device_id_type=MESH,
    )
    loads = []
    for a in range(4):
        for side in range(2):
            lanes = pl.ds(side * EAST, EAST)
            loads.append(
                pltpu.make_async_copy(
                    fields[a].at[:, :, lanes],
                    held.at[a, pl.ds(16 * side, 16), :, lanes],
                    load_sem.at[a, side],
                )
            )

    pl.semaphore_wait(barrier, 31)

    @pl.loop(0, CHUNKS)
    def _(c):
        for a in range(4):
            for side in range(2):
                in_copy(side, a, c).start()

    second_copy.start()
    for copy in loads:
        copy.start()
    for copy in small:
        copy.wait()
    seconds_ref[t] = second_ref[...]

    lat_shift, lon_shift = shifts_ref[0], shifts_ref[1]
    w, n = iota((128, 256), 0), iota((128, 256), 1)
    same = (lat_shift + w // 8) % 16 == (n // 8) % 16
    gather[...] = onehot(same & (w % 8 + lon_shift == n % 8 + 8 * (n // 128)))
    n, w = iota((256, 128), 0), iota((256, 128), 1)
    same = (lat_shift + w // 8) % 16 == (n // 8) % 16
    place[...] = onehot(same & (w % 8 + lon_shift == n % 8 + 8 * (n // 128)))

    pre, _, _ = hidden_before(layer_ref[0:2, :], layer_ref[2:3, :])
    logits = dot(second_ref[...], jnp.maximum(pre, 0.0), 1, 1, HIGHEST)
    table = jnp.where(used_bins(HEADS), 16.0 * jax.nn.sigmoid(logits), 0.0)
    table = three_parts(jnp.concatenate([table, jnp.zeros((4, 256), F32)], axis=0))
    b, l = iota((256, 128), 0), iota((256, 128), 1)
    for cj in range(8):
        here = (b == (l // 8) * 16 + (l % 8 - cj + 16) % 16) | (b == 8) | (b == 24)
        sel = onehot(here)
        expand[:, cj * 128 : (cj + 1) * 128] = sel
        wide = dot(table, sel, 1, 0)
        wide = wide[0:24] + wide[24:48] + wide[48:72]
        rows[pl.ds(cj, HEADS, stride=8), :] = wide[0:HEADS]

    j, l = iota((64, 128), 0), iota((64, 128), 1)
    land = land_ref[...].astype(F32).astype(BF16)
    for side in range(2):
        g, l = iota((256, 128), 0), iota((256, 128), 1)
        first_col = (sp + 31 * side) * 8 + lon_shift
        land_cols = dot(land, onehot(g == (first_col + l) % 256), 1, 0).astype(BF16)
        j, l = iota((64, 128), 0), iota((64, 128), 1)
        halves = []
        for blk in range(2):
            jj, lat = iota((64, 16), 0), iota((64, 16), 1)
            pick = onehot(lat == (lat_shift + jj // 8 + 8 * blk) % 16)
            spread = dot(pick, land_cols, 1, 0)
            halves.append(jnp.sum(jnp.where(l == j % 8, spread, 0.0), axis=1, keepdims=True))
        is_land[side] = jnp.where(l < 64, halves[0], halves[1])
    apart = (l >= 64) & ((j // 8 < 8 - lat_shift) != ((l % 64) // 8 < 8 - lat_shift))
    masked = jnp.where(apart, MASKED * LOG2E, 0.0)

    for side in range(2):

        @pl.loop(side * HALF, side * HALF + HALF)
        def _(h):
            one = rows[pl.ds(pl.multiple_of(h * 8, 8), 8), :]
            lane = iota((8, 128), 1)
            low, high = keybias_ref[0, h] * LOG2E, keybias_ref[1, h] * LOG2E
            for rj in range(8):
                left = pltpu.roll(one, 8 * rj, 1) if rj else one
                right = pltpu.roll(one, 8 * rj + 64, 1)
                at = slice(8 * rj, 8 * rj + 8)
                key = jnp.where(is_land[side, at] > 0.5, high, low) + masked[at]
                bias[h, at, :] = jnp.where(lane < 64, left, right) * LOG2E + key

    for copy in loads:
        copy.wait()
    scale = 128.0 ** -0.5

    @pl.loop(0, CHUNKS)
    def _(c):
        front = iota((64, 128), 1) < 64

        def paired(x):
            return jnp.where(front, x[0:64], x[64:128])

        def split(x):
            return jnp.concatenate(
                [jnp.where(front, x, 0.0), jnp.where(front, 0.0, x)], axis=0
            ).astype(BF16)

        for side in range(2):
            for a in range(4):
                in_copy(side, a, c).wait_recv()
        merged = []
        for side in range(2):
            lanes = lanes_of(side, c)
            for a in range(4):
                both = held[a, :, :, lanes].reshape(256, LANES)
                merged.append(dot(gather[...], both, 1, 0).astype(BF16))
        work = []
        for side in range(2):
            for i in range(PAIR):
                s = slice(128 * i, 128 * i + 128)
                work.append((side, side * HALF + c * PAIR + i, [merged[side * 4 + a][:, s] for a in range(4)]))
        scores = [paired(dot(f[1], f[0], 1, 1)) for _, _, f in work]
        dprobs = [paired(dot(f[2], f[3], 1, 1)) for _, _, f in work]
        probs, dscores = [], []
        for (side, h, _), score, dprob in zip(work, scores, dprobs):
            sc = score * (scale * LOG2E) + bias[h]
            e = jnp.exp2(sc - jnp.max(sc, axis=0, keepdims=True))
            p = e * (1.0 / jnp.sum(e, axis=0, keepdims=True))
            pd = p * dprob
            probs.append(p)
            dscores.append(pd - p * jnp.sum(pd, axis=0, keepdims=True))
        lane8 = iota((8, 128), 1)
        for (side, h, _), ds in zip(work, dscores):
            acc = jnp.zeros((8, 128), F32)
            land_acc = jnp.zeros((8, 128), F32)
            for rj in range(8):
                at = slice(8 * rj, 8 * rj + 8)
                part = ds[at]
                land_acc += part * is_land[side, at]
                both = jnp.where(lane8 < 64, part + pltpu.roll(part, 64, 1), 0.0)
                acc += pltpu.roll(both, 128 - 8 * rj, 1) if rj else both
            at = pl.ds(pl.multiple_of(h * 8, 8), 8)
            rows[at, :] = acc
            land_rows[at, :] = land_acc
        grads = []
        for (side, h, f), p, ds in zip(work, probs, dscores):
            p_low, ds_low = split(p), split(ds)
            grads.append(
                (
                    dot(ds_low, f[1], 0, 0) * scale,
                    dot(ds_low, f[0], 1, 0) * scale,
                    dot(p_low, f[3], 1, 0),
                )
            )
        for side in range(2):
            lanes = lanes_of(side, c)
            for a in range(3):
                value = jnp.concatenate(
                    [grads[side * PAIR + i][a] for i in range(PAIR)], axis=1
                ).astype(BF16)
                placed = dot(place[...], value, 1, 0).astype(BF16)
                here = placed[128 * side : 128 * side + 128]
                there = placed[128 - 128 * side : 256 - 128 * side]
                out_ref[a, :, :, lanes] = here.reshape(16, 8, LANES)
                far[a, :, :, lanes] = there.reshape(16, 8, LANES)
            back_copy(side, c).start()

    pad = jnp.zeros((4, 1024), F32)
    flat = jnp.concatenate([rows[pl.ds(cj, HEADS, stride=8), :] for cj in range(8)], axis=1)
    land_flat = jnp.concatenate(
        [land_rows[pl.ds(cj, HEADS, stride=8), :] for cj in range(8)], axis=1
    )
    stacked = three_parts(jnp.concatenate([flat, pad, land_flat, pad], axis=0))
    binned = dot(stacked, expand[...], 1, 1)
    binned = binned[0:48] + binned[48:96] + binned[96:144]
    binned = jnp.where(iota((24, 256), 1) == 24, binned[24:48], binned[0:24])
    for i in range(6):
        table_part[i] = binned[(i // 2) * 8 : (i // 2) * 8 + 8, (i % 2) * 128 : (i % 2) * 128 + 128]
    table_part[6:8] = jnp.zeros((2, 8, 128), F32)

    def exchange(pieces):
        return [
            pltpu.make_async_remote_copy(
                src_ref=src,
                dst_ref=dst,
                send_sem=send.at[i],
                recv_sem=recv.at[i],
                device_id=to,
                device_id_type=MESH,
            )
            for i, (src, dst, send, recv, to) in enumerate(pieces)
        ]

    def add_arrived(c):
        for side in range(2):
            lanes = lanes_of(side, c)
            back_copy(side, c).wait_recv()
            for a in range(3):
                out_ref[a, :, :, lanes] = out_ref[a, :, :, lanes] + arrived[a, :, :, lanes]

    slot = x_lo * 4 + y
    copies = exchange(
        [(table_part.at[i], near_part.at[slot * 2 + core], near_send, near_recv, to) for i, to in near]
    )
    for copy in copies:
        copy.start()
    near_part[slot * 2 + core] = table_part[slot]
    for copy in copies:
        copy.wait()
    mine = near_part[0]
    for i in range(1, 16):
        mine = mine + near_part[i]

    z_part[z] = mine
    copies = exchange([(z_part.at[z], z_part.at[z], z_send, z_recv, to) for to in z_ids])
    for copy in copies:
        copy.start()

    @pl.loop(0, 2)
    def _(c):
        add_arrived(c)

    for copy in copies:
        copy.wait()
    mine = z_part[0]
    for i in range(1, 8):
        mine = mine + z_part[i]

    sums_ref[x * 4 + y] = mine
    here = sums_ref.at[x * 4 + y]
    copies = exchange([(here, here, xy_send, xy_recv, to) for to in xy_ids])
    for copy in copies:
        copy.start()

    @pl.loop(2, CHUNKS)
    def _(c):
        add_arrived(c)

    second_copy.wait()

    @pl.loop(0, CHUNKS)
    def _(c):
        for side in range(2):
            for a in range(4):
                in_copy(side, a, c).wait_send()
            back_copy(side, c).wait_send()

    for copy in copies:
        copy.wait()


def last_kernel(
    grads_ref,
    sums_hbm,
    seconds_hbm,
    layer_hbm,
    gq_ref,
    gk_ref,
    gv_ref,
    gfirst_ref,
    goffset_ref,
    gsecond_ref,
    gkey_ref,
    sums_ref,
    seconds_ref,
    layer_ref,
    held,
    sem,
):
    small = [
        pltpu.make_async_copy(a, b, sem.at[3 + i])
        for i, (a, b) in enumerate(
            ((layer_hbm, layer_ref), (seconds_hbm, seconds_ref), (sums_hbm, sums_ref))
        )
    ]
    for copy in small:
        copy.start()
    outs = (gq_ref, gk_ref, gv_ref)
    loads = [pltpu.make_async_copy(grads_ref.at[a], held.at[a], sem.at[6 + a]) for a in range(3)]
    copies = [pltpu.make_async_copy(held.at[a], outs[a], sem.at[a]) for a in range(3)]
    for copy in loads:
        copy.start()
    for copy in small:
        copy.wait()
    for load, copy in zip(loads, copies):
        load.wait()
        copy.start()
    t = lax.axis_index("tensor")
    pre, cy, cx = hidden_before(layer_ref[0:2, :], layer_ref[2:3, :])
    hidden = jnp.maximum(pre, 0.0)

    def bins(half):
        strips = [
            jnp.concatenate([sums_ref[half * 8 + 2 * i], sums_ref[half * 8 + 2 * i + 1]], axis=1)
            for i in range(3)
        ]
        return jnp.concatenate(strips, axis=0)

    def pulled(half):
        logits = dot(seconds_ref[half], hidden, 1, 1, HIGHEST)
        p = jax.nn.sigmoid(logits)
        return jnp.where(used_bins(HEADS), bins(half)[0:HEADS] * (16.0 * p * (1.0 - p)), 0.0)

    low, high = pulled(0), pulled(1)
    mine = jnp.where(t == 0, low, high)
    gsecond_ref[...] = dot(mine, hidden, 1, 0, HIGHEST)
    ghidden = dot(low, seconds_ref[0], 0, 0, HIGHEST) + dot(high, seconds_ref[1], 0, 0, HIGHEST)
    ghidden = jnp.where(pre > 0.0, ghidden, 0.0)
    gfirst_ref[0:1, :] = jnp.sum(cy * ghidden, axis=0, keepdims=True)
    gfirst_ref[1:2, :] = jnp.sum(cx * ghidden, axis=0, keepdims=True)
    goffset_ref[...] = jnp.sum(ghidden, axis=0, keepdims=True)
    r, n = iota((8, 256), 0), iota((8, 256), 1)
    pick = jnp.where(n == 24, jnp.where(r == 0, -1.0, 1.0), jnp.where((n == 8) & (r == 0), 1.0, 0.0))
    keys = dot(pick, jnp.where(t == 0, bins(0), bins(1)), 1, 1, HIGHEST)
    gkey_ref[...] = keys[0:2, 0:HEADS]
    for copy in copies:
        copy.wait()


def on_device(q, k, v, d, land, shifts, first, offset, second, keybias):
    shape = q.shape
    field = (16, 8, HEADS * 128)
    fields = [a.reshape(field) for a in (q, k, v, d)]
    vmem = pl.BlockSpec(memory_space=pltpu.VMEM)
    hbm = pl.BlockSpec(memory_space=pltpu.HBM)
    dma = pltpu.SemaphoreType.DMA
    vec = pltpu.VMEM
    outs = pl.pallas_call(
        main_kernel,
        out_shape=(
            jax.ShapeDtypeStruct((3,) + field, BF16),
            jax.ShapeDtypeStruct((16, 8, 128), F32),
            jax.ShapeDtypeStruct((2, HEADS, 512), F32),
            jax.ShapeDtypeStruct((3, 512), F32),
        ),
        in_specs=[hbm] * 10,
        out_specs=(vmem,) * 4,
        scratch_shapes=[
            vec((4, 32, 8, HEADS * 128), BF16),
            vec((3,) + field, BF16),
            vec((3,) + field, BF16),
            vec((HEADS, 64, 128), F32),
            vec((256, 1024), BF16),
            vec((HEADS * 8, 128), F32),
            vec((HEADS * 8, 128), F32),
            vec((2, 64, 128), F32),
            vec((128, 256), BF16),
            vec((256, 128), BF16),
            vec((8, 8, 128), F32),
            vec((16, 8, 128), F32),
            vec((8, 8, 128), F32),
            vec((16, 256), jnp.int32),
            vec((HEADS, 512), F32),
            pltpu.SMEM((2,), jnp.int32),
            pltpu.SMEM((2, HEADS), F32),
            dma((4, 2)),
            dma((6,)),
            dma((2, 4, CHUNKS)),
            dma((2, 4, CHUNKS)),
            dma((2, CHUNKS)),
            dma((2, CHUNKS)),
            dma((2,)),
            dma((15,)),
            dma((15,)),
            dma((7,)),
            dma((7,)),
            dma((15,)),
            dma((15,)),
        ],
        compiler_params=pltpu.CompilerParams(
            collective_id=0, has_side_effects=True, vmem_limit_bytes=60 * 2**20
        ),
        name="exchange_and_grads",
    )(*fields, land, shifts, first, offset.reshape(1, 512), second.T, keybias)
    gq, gk, gv, gfirst, goffset, gsecond, gkey = pl.pallas_call(
        last_kernel,
        out_shape=(jax.ShapeDtypeStruct(field, BF16),) * 3
        + (
            jax.ShapeDtypeStruct((2, 512), F32),
            jax.ShapeDtypeStruct((1, 512), F32),
            jax.ShapeDtypeStruct((HEADS, 512), F32),
            jax.ShapeDtypeStruct((2, HEADS), F32),
        ),
        in_specs=[hbm] * 4,
        out_specs=(hbm,) * 3 + (vmem,) * 4,
        scratch_shapes=[
            vec((16, 8, 128), F32),
            vec((2, HEADS, 512), F32),
            vec((3, 512), F32),
            vec((3,) + field, BF16),
            dma((9,)),
        ],
        compiler_params=pltpu.CompilerParams(vmem_limit_bytes=60 * 2**20),
        name="write_and_reduce",
    )(*outs)
    return (
        gq.reshape(shape),
        gk.reshape(shape),
        gv.reshape(shape),
        gfirst,
        goffset.reshape(512),
        gsecond.T,
        gkey,
    )


def solution(mesh):
    field = P("dp", None, "space", "tensor")
    second = P(None, "tensor")
    return jax.shard_map(
        on_device,
        mesh=mesh,
        in_specs=(field,) * 4 + (P(), P(), P(), P(), second, second),
        out_specs=(field,) * 3 + (P(), P(), second, second),
        check_vma=False,
    )
```

profile of v0, /device:TPU:1, one launch (start us, length us, event | category | flops | bytes accessed | tf_op | source)
XLA Modules:
  0.0 55.9 jit_solution(1176814085633391809)
XLA Ops:
  0.6 50.8 %exchange_and_grads.1 = (bf16[3,16,8,2560]{3,2,1,0:T(8,128)(2,1)}, f32[16,8,128]{2,1,0:T(8,128)}, f32[2,20,512]{2,1,0:T(8,128)}, f32[3,512]{1,0:T(4,128)}) custom-call(bf16[16,8,2560]{2,1,0:T(8,128)(2,1)} %bitcast.11, bf16[16,8,2560]{2,1,0:T(8,128)(2,1)} %bitcast.12, bf16[16,8,2560]{2,1,0:T(8,128)(2,1)} %bitcast.13, bf16[16,8,2560]{2,1,0:T(8,128)(2,1)} %bitcast.14, ...), custom_call_target="tpu_custom_call" | custom-call | tf_op jit(solution)/shard_map/exchange_and_grads/pallas_call | solution.py:501
  51.4 4.5 %write_and_reduce.1 = (bf16[16,8,2560]{2,1,0:T(8,128)(2,1)}, bf16[16,8,2560]{2,1,0:T(8,128)(2,1)}, bf16[16,8,2560]{2,1,0:T(8,128)(2,1)}, f32[2,512]{1,0:T(2,128)...) custom-call(bf16[3,16,8,2560]{3,2,1,0:T(8,128)(2,1)} %get-tuple-element.18.grads_ref, ...), custom_call_target="tpu_custom_call" | custom-call | tf_op jit(solution)/shard_map/write_and_reduce/pallas_call | solution.py:548
where the time goes:
time: 56.5 us; the launch traced here: 55.9 us
  Pallas kernels  55.3 us (98%)
  between operations  0.64 us (1%)
    pallas_call x1, Pallas kernels, on_device(): pl.pallas_call(main_kernel, out_shape=(jax.ShapeDtypeStruct((3,) + field,...  50.8 us
    pallas_call x1, Pallas kernels, on_device(): pl.pallas_call(last_kernel, out_shape=(jax.ShapeDtypeStruct(field, BF16),...  4.52 us

commit v1 on v0

--- a/solution.py
+++ b/solution.py
@@ -9,11 +9,12 @@
 MASKED = -1000000000.0
 LOG2E = 1.4426950408889634
 HEADS = 20
-HALF = HEADS // 2
-PAIR = 2
-CHUNKS = HALF // PAIR
-LANES = PAIR * 128
-EAST = HALF * 128
+GROUP = 4
+CHUNKS = HEADS // GROUP
+LANES = GROUP * 128
+ROOM = 9
+SIDE = ROOM * 16
+BOTH = 2 * SIDE
 BF16 = jnp.bfloat16
 F32 = jnp.float32
 HIGHEST = lax.Precision.HIGHEST
@@ -58,6 +59,29 @@
     b = rest.astype(BF16)
     c = (rest - b.astype(F32)).astype(BF16)
     return jnp.concatenate([a, b, c], axis=0)
+
+
+def west_heads(shift):
+    return jnp.where(shift <= 2, 4, jnp.where(shift >= 6, 0, 6 - shift))
+
+
+def block_of(head, column, shift, west):
+    return jnp.where(
+        head < west, head * shift + column, ROOM + (head - west) * (8 - shift) + column - shift
+    )
+
+
+def patch_code(head, n, shift, west):
+    lat, column = n // 8, n % 8
+    leaves = (head < west) == (column < shift)
+    return jnp.where(leaves, block_of(head, column, shift, west) * 16 + lat, -1)
+
+
+def window_place(head, w, shift, lat_shift, west):
+    lat = (lat_shift + w // 8) % 16
+    column = w % 8 + shift
+    over = column >= 8
+    return over == (head < west), jnp.where(over, column - 8, column), lat
 
 
 def main_kernel(
@@ -76,6 +100,10 @@
     seconds_ref,
     layer_ref,
     held,
+    own,
+    packed,
+    lent,
+    window,
     far,
     arrived,
     bias,
@@ -83,7 +111,9 @@
     rows,
     land_rows,
     is_land,
-    gather,
+    pack_in,
+    pack_back,
+    merge,
     place,
     table_part,
     near_part,
@@ -129,10 +159,6 @@
         other_ids.append({"dp": yy, "space": xx * 16 + z * 2 + core, "tensor": 1 - t})
     tensor_id = {"tensor": 1 - t}
 
-    barrier = pltpu.get_barrier_semaphore()
-    for to in [slow_id] + [i for _, i in near] + z_ids + other_ids:
-        pl.semaphore_signal(barrier, inc=1, device_id=to, device_id_type=MESH)
-
     fields = (q_ref, k_ref, v_ref, d_ref)
     small = [
         pltpu.make_async_copy(a, b, small_sem.at[i])
@@ -147,28 +173,34 @@
             )
         )
     ]
-    for copy in small:
-        copy.start()
-
-    def lanes_of(side, c):
-        return pl.ds(pl.multiple_of(side * EAST + c * LANES, LANES), LANES)
-
-    def in_copy(side, a, c):
-        lanes = lanes_of(side, c)
+    loads = [pltpu.make_async_copy(ref, held.at[a], load_sem.at[a]) for a, ref in enumerate(fields)]
+    small[0].start()
+    for copy in loads:
+        copy.start()
+    for copy in small[1:]:
+        copy.start()
+
+    barrier = pltpu.get_barrier_semaphore()
+    for to in [slow_id] + [i for _, i in near] + z_ids + other_ids:
+        pl.semaphore_signal(barrier, inc=1, device_id=to, device_id_type=MESH)
+
+    def side_rows(side):
+        return pl.ds(side * SIDE, SIDE)
+
+    def in_copy(side, c):
         return pltpu.make_async_remote_copy(
-            src_ref=fields[a].at[:, :, lanes],
-            dst_ref=held.at[a, pl.ds(16 - 16 * side, 16), :, lanes],
-            send_sem=in_send.at[side, a, c],
-            recv_sem=in_recv.at[side, a, c],
+            src_ref=packed.at[c, side_rows(side)],
+            dst_ref=lent.at[c, side_rows(side)],
+            send_sem=in_send.at[side, c],
+            recv_sem=in_recv.at[side, c],
             device_id=east_id if side else west_id,
             device_id_type=MESH,
         )
 
     def back_copy(side, c):
-        lanes = lanes_of(side, c)
         return pltpu.make_async_remote_copy(
-            src_ref=far.at[:, :, :, lanes],
-            dst_ref=arrived.at[:, :, :, lanes],
+            src_ref=far.at[c, side_rows(side)],
+            dst_ref=arrived.at[c, side_rows(side)],
             send_sem=back_send.at[side, c],
             recv_sem=back_recv.at[side, c],
             device_id=west_id if side else east_id,
@@ -183,40 +215,53 @@
         device_id=tensor_id,
         device_id_type=MESH,
     )
-    loads = []
-    for a in range(4):
+
+    small[0].wait()
+    lat_shift, shift = shifts_ref[0], shifts_ref[1]
+    west = west_heads(shift)
+    e = iota((1, GROUP * 128), 1)
+    code = patch_code(e // 128, e % 128, shift, west)
+    pack_in[...] = onehot(iota((BOTH, GROUP * 128), 0) == code)
+
+    def pack(c):
+        for i in range(GROUP):
+            lanes = pl.ds(pl.multiple_of(c * LANES, LANES) + 128 * i, 128)
+            for a in range(4):
+                own[c, 128 * i : 128 * i + 128, 128 * a : 128 * a + 128] = held[
+                    a, :, :, lanes
+                ].reshape(128, 128)
+        packed[c] = dot(pack_in[...], own[c], 1, 0).astype(BF16)
+
+    for copy in loads:
+        copy.wait()
+    pack(0)
+    pl.semaphore_wait(barrier, 31)
+    for side in range(2):
+        in_copy(side, 0).start()
+
+    @pl.loop(1, CHUNKS)
+    def _(c):
+        pack(c)
         for side in range(2):
-            lanes = pl.ds(side * EAST, EAST)
-            loads.append(
-                pltpu.make_async_copy(
-                    fields[a].at[:, :, lanes],
-                    held.at[a, pl.ds(16 * side, 16), :, lanes],
-                    load_sem.at[a, side],
-                )
-            )
-
-    pl.semaphore_wait(barrier, 31)
-
-    @pl.loop(0, CHUNKS)
-    def _(c):
-        for a in range(4):
-            for side in range(2):
-                in_copy(side, a, c).start()
+            in_copy(side, c).start()
 
     second_copy.start()
-    for copy in loads:
-        copy.start()
-    for copy in small:
+    for copy in small[1:]:
         copy.wait()
     seconds_ref[t] = second_ref[...]
 
-    lat_shift, lon_shift = shifts_ref[0], shifts_ref[1]
-    w, n = iota((128, 256), 0), iota((128, 256), 1)
-    same = (lat_shift + w // 8) % 16 == (n // 8) % 16
-    gather[...] = onehot(same & (w % 8 + lon_shift == n % 8 + 8 * (n // 128)))
-    n, w = iota((256, 128), 0), iota((256, 128), 1)
-    same = (lat_shift + w // 8) % 16 == (n // 8) % 16
-    place[...] = onehot(same & (w % 8 + lon_shift == n % 8 + 8 * (n // 128)))
+    borrowed, column, lat = window_place(e // 128, e % 128, shift, lat_shift, west)
+    code = jnp.where(borrowed, block_of(e // 128, column, shift, west) * 16 + lat, -1)
+    pack_back[...] = onehot(iota((BOTH, GROUP * 128), 0) == code)
+    for i in range(GROUP):
+        n, target = iota((128, 1), 0), iota((128, 128 + BOTH), 1)
+        borrowed, column, lat = window_place(i, n, shift, lat_shift, west)
+        code = block_of(i, column, shift, west) * 16 + lat
+        merge[i] = onehot(target == jnp.where(borrowed, 128 + code, lat * 8 + column))
+        code = patch_code(i, n, shift, west)
+        row = (n // 8 + 16 - lat_shift) % 16
+        here = row * 8 + (n % 8 + 8 - shift) % 8
+        place[i] = onehot(target == jnp.where(code >= 0, 128 + code, here))
 
     pre, _, _ = hidden_before(layer_ref[0:2, :], layer_ref[2:3, :])
     logits = dot(second_ref[...], jnp.maximum(pre, 0.0), 1, 1, HIGHEST)
@@ -231,39 +276,39 @@
         wide = wide[0:24] + wide[24:48] + wide[48:72]
         rows[pl.ds(cj, HEADS, stride=8), :] = wide[0:HEADS]
 
+    land = land_ref[...].astype(F32).astype(BF16)
     j, l = iota((64, 128), 0), iota((64, 128), 1)
-    land = land_ref[...].astype(F32).astype(BF16)
+    lands = []
     for side in range(2):
-        g, l = iota((256, 128), 0), iota((256, 128), 1)
-        first_col = (sp + 31 * side) * 8 + lon_shift
-        land_cols = dot(land, onehot(g == (first_col + l) % 256), 1, 0).astype(BF16)
-        j, l = iota((64, 128), 0), iota((64, 128), 1)
+        g, cols = iota((256, 128), 0), iota((256, 128), 1)
+        first_col = (sp + 31 * side) * 8 + shift
+        land_cols = dot(land, onehot(g == (first_col + cols) % 256), 1, 0).astype(BF16)
         halves = []
         for blk in range(2):
             jj, lat = iota((64, 16), 0), iota((64, 16), 1)
             pick = onehot(lat == (lat_shift + jj // 8 + 8 * blk) % 16)
             spread = dot(pick, land_cols, 1, 0)
             halves.append(jnp.sum(jnp.where(l == j % 8, spread, 0.0), axis=1, keepdims=True))
-        is_land[side] = jnp.where(l < 64, halves[0], halves[1])
+        lands.append(jnp.where(l < 64, halves[0], halves[1]))
+    for i in range(GROUP):
+        is_land[i] = jnp.where(i < west, lands[0], lands[1])
     apart = (l >= 64) & ((j // 8 < 8 - lat_shift) != ((l % 64) // 8 < 8 - lat_shift))
     masked = jnp.where(apart, MASKED * LOG2E, 0.0)
 
-    for side in range(2):
-
-        @pl.loop(side * HALF, side * HALF + HALF)
-        def _(h):
+    @pl.loop(0, CHUNKS)
+    def _(c):
+        lane = iota((8, 128), 1)
+        for i in range(GROUP):
+            h = c * GROUP + i
             one = rows[pl.ds(pl.multiple_of(h * 8, 8), 8), :]
-            lane = iota((8, 128), 1)
             low, high = keybias_ref[0, h] * LOG2E, keybias_ref[1, h] * LOG2E
             for rj in range(8):
                 left = pltpu.roll(one, 8 * rj, 1) if rj else one
                 right = pltpu.roll(one, 8 * rj + 64, 1)
                 at = slice(8 * rj, 8 * rj + 8)
-                key = jnp.where(is_land[side, at] > 0.5, high, low) + masked[at]
+                key = jnp.where(is_land[i, at] > 0.5, high, low) + masked[at]
                 bias[h, at, :] = jnp.where(lane < 64, left, right) * LOG2E + key
 
-    for copy in loads:
-        copy.wait()
     scale = 128.0 ** -0.5
 
     @pl.loop(0, CHUNKS)
@@ -279,63 +324,44 @@
             ).astype(BF16)
 
         for side in range(2):
-            for a in range(4):
-                in_copy(side, a, c).wait_recv()
+            in_copy(side, c).wait_recv()
+        theirs = lent[c]
         merged = []
-        for side in range(2):
-            lanes = lanes_of(side, c)
-            for a in range(4):
-                both = held[a, :, :, lanes].reshape(256, LANES)
-                merged.append(dot(gather[...], both, 1, 0).astype(BF16))
-        work = []
-        for side in range(2):
-            for i in range(PAIR):
-                s = slice(128 * i, 128 * i + 128)
-                work.append((side, side * HALF + c * PAIR + i, [merged[side * 4 + a][:, s] for a in range(4)]))
-        scores = [paired(dot(f[1], f[0], 1, 1)) for _, _, f in work]
-        dprobs = [paired(dot(f[2], f[3], 1, 1)) for _, _, f in work]
+        for i in range(GROUP):
+            both = jnp.concatenate([own[c, 128 * i : 128 * i + 128, :], theirs], axis=0)
+            whole = dot(merge[i], both, 1, 0).astype(BF16)
+            merged.append([whole[:, 128 * a : 128 * a + 128] for a in range(4)])
+        scores = [paired(dot(f[1], f[0], 1, 1)) for f in merged]
+        dprobs = [paired(dot(f[2], f[3], 1, 1)) for f in merged]
         probs, dscores = [], []
-        for (side, h, _), score, dprob in zip(work, scores, dprobs):
-            sc = score * (scale * LOG2E) + bias[h]
+        for i in range(GROUP):
+            sc = scores[i] * (scale * LOG2E) + bias[c * GROUP + i]
             e = jnp.exp2(sc - jnp.max(sc, axis=0, keepdims=True))
             p = e * (1.0 / jnp.sum(e, axis=0, keepdims=True))
-            pd = p * dprob
+            pd = p * dprobs[i]
             probs.append(p)
             dscores.append(pd - p * jnp.sum(pd, axis=0, keepdims=True))
         lane8 = iota((8, 128), 1)
-        for (side, h, _), ds in zip(work, dscores):
+        for i in range(GROUP):
             acc = jnp.zeros((8, 128), F32)
             land_acc = jnp.zeros((8, 128), F32)
             for rj in range(8):
                 at = slice(8 * rj, 8 * rj + 8)
-                part = ds[at]
-                land_acc += part * is_land[side, at]
+                part = dscores[i][at]
+                land_acc += part * is_land[i, at]
                 both = jnp.where(lane8 < 64, part + pltpu.roll(part, 64, 1), 0.0)
                 acc += pltpu.roll(both, 128 - 8 * rj, 1) if rj else both
-            at = pl.ds(pl.multiple_of(h * 8, 8), 8)
+            at = pl.ds(pl.multiple_of((c * GROUP + i) * 8, 8), 8)
             rows[at, :] = acc
             land_rows[at, :] = land_acc
-        grads = []
-        for (side, h, f), p, ds in zip(work, probs, dscores):
-            p_low, ds_low = split(p), split(ds)
-            grads.append(
-                (
-                    dot(ds_low, f[1], 0, 0) * scale,
-                    dot(ds_low, f[0], 1, 0) * scale,
-                    dot(p_low, f[3], 1, 0),
-                )
-            )
+        for i in range(GROUP):
+            f, at = merged[i], slice(128 * i, 128 * i + 128)
+            p_low, ds_low = split(probs[i]), split(dscores[i])
+            window[c, at, 0:128] = (dot(ds_low, f[1], 0, 0) * scale).astype(BF16)
+            window[c, at, 128:256] = (dot(ds_low, f[0], 1, 0) * scale).astype(BF16)
+            window[c, at, 256:384] = dot(p_low, f[3], 1, 0).astype(BF16)
+        far[c] = dot(pack_back[...], window[c], 1, 0).astype(BF16)
         for side in range(2):
-            lanes = lanes_of(side, c)
-            for a in range(3):
-                value = jnp.concatenate(
-                    [grads[side * PAIR + i][a] for i in range(PAIR)], axis=1
-                ).astype(BF16)
-                placed = dot(place[...], value, 1, 0).astype(BF16)
-                here = placed[128 * side : 128 * side + 128]
-                there = placed[128 - 128 * side : 256 - 128 * side]
-                out_ref[a, :, :, lanes] = here.reshape(16, 8, LANES)
-                far[a, :, :, lanes] = there.reshape(16, 8, LANES)
             back_copy(side, c).start()
 
     pad = jnp.zeros((4, 1024), F32)
@@ -364,12 +390,16 @@
             for i, (src, dst, send, recv, to) in enumerate(pieces)
         ]
 
-    def add_arrived(c):
+    def finish(c):
         for side in range(2):
-            lanes = lanes_of(side, c)
             back_copy(side, c).wait_recv()
+        theirs = arrived[c]
+        for i in range(GROUP):
+            lanes = pl.ds(pl.multiple_of(c * LANES, LANES) + 128 * i, 128)
+            both = jnp.concatenate([window[c, 128 * i : 128 * i + 128, :], theirs], axis=0)
+            whole = dot(place[i], both, 1, 0).astype(BF16)
             for a in range(3):
-                out_ref[a, :, :, lanes] = out_ref[a, :, :, lanes] + arrived[a, :, :, lanes]
+                out_ref[a, :, :, lanes] = whole[:, 128 * a : 128 * a + 128].reshape(16, 8, 128)
 
     slot = x_lo * 4 + y
     copies = exchange(
@@ -391,7 +421,7 @@
 
     @pl.loop(0, 2)
     def _(c):
-        add_arrived(c)
+        finish(c)
 
     for copy in copies:
         copy.wait()
@@ -407,15 +437,14 @@
 
     @pl.loop(2, CHUNKS)
     def _(c):
-        add_arrived(c)
+        finish(c)
 
     second_copy.wait()
 
     @pl.loop(0, CHUNKS)
     def _(c):
         for side in range(2):
-            for a in range(4):
-                in_copy(side, a, c).wait_send()
+            in_copy(side, c).wait_send()
             back_copy(side, c).wait_send()
 
     for copy in copies:
@@ -509,16 +538,22 @@
         in_specs=[hbm] * 10,
         out_specs=(vmem,) * 4,
         scratch_shapes=[
-            vec((4, 32, 8, HEADS * 128), BF16),
-            vec((3,) + field, BF16),
-            vec((3,) + field, BF16),
+            vec((4,) + field, BF16),
+            vec((CHUNKS, GROUP * 128, 512), BF16),
+            vec((CHUNKS, BOTH, 512), BF16),
+            vec((CHUNKS, BOTH, 512), BF16),
+            vec((CHUNKS, GROUP * 128, 384), BF16),
+            vec((CHUNKS, BOTH, 384), BF16),
+            vec((CHUNKS, BOTH, 384), BF16),
             vec((HEADS, 64, 128), F32),
             vec((256, 1024), BF16),
             vec((HEADS * 8, 128), F32),
             vec((HEADS * 8, 128), F32),
-            vec((2, 64, 128), F32),
-            vec((128, 256), BF16),
-            vec((256, 128), BF16),
+            vec((GROUP, 64, 128), F32),
+            vec((BOTH, GROUP * 128), BF16),
+            vec((BOTH, GROUP * 128), BF16),
+            vec((GROUP, 128, 128 + BOTH), BF16),
+            vec((GROUP, 128, 128 + BOTH), BF16),
             vec((8, 8, 128), F32),
             vec((16, 8, 128), F32),
             vec((8, 8, 128), F32),
@@ -526,10 +561,10 @@
             vec((HEADS, 512), F32),
             pltpu.SMEM((2,), jnp.int32),
             pltpu.SMEM((2, HEADS), F32),
-            dma((4, 2)),
+            dma((4,)),
             dma((6,)),
-            dma((2, 4, CHUNKS)),
-            dma((2, 4, CHUNKS)),
+            dma((2, CHUNKS)),
+            dma((2, CHUNKS)),
             dma((2, CHUNKS)),
             dma((2, CHUNKS)),
             dma((2,)),

time: 56.5 us -> 45.4 us (0.80)
  Pallas kernels: 55.3 us -> 44.4 us
    pallas_call x1, Pallas kernels: 50.8 us -> 39.9 us  [on_device(): pl.pallas_call(main_kernel, out_shape=(jax.ShapeDtypeStruct((3,) + field,...]
where the time goes in v1:
time: 45.4 us; the launch traced here: 45.1 us
  Pallas kernels  44.4 us (98%)
  between operations  0.64 us (1%)
    pallas_call x1, Pallas kernels, on_device(): pl.pallas_call(main_kernel, out_shape=(jax.ShapeDtypeStruct((3,) + field,...  39.9 us
    pallas_call x1, Pallas kernels, on_device(): pl.pallas_call(last_kernel, out_shape=(jax.ShapeDtypeStruct(field, BF16),...  4.52 us

profile of v1, /device:TPU:1, one launch (start us, length us, event | category | flops | bytes accessed | tf_op | source)
XLA Modules:
  0.0 45.1 jit_solution(3464491079229036212)
XLA Ops:
  0.6 39.9 %exchange_and_grads.1 = (bf16[3,16,8,2560]{3,2,1,0:T(8,128)(2,1)}, f32[16,8,128]{2,1,0:T(8,128)}, f32[2,20,512]{2,1,0:T(8,128)}, f32[3,512]{1,0:T(4,128)}) custom-call(bf16[16,8,2560]{2,1,0:T(8,128)(2,1)} %bitcast.11, bf16[16,8,2560]{2,1,0:T(8,128)(2,1)} %bitcast.12, bf16[16,8,2560]{2,1,0:T(8,128)(2,1)} %bitcast.13, bf16[16,8,2560]{2,1,0:T(8,128)(2,1)} %bitcast.14, ...), custom_call_target="tpu_custom_call" | custom-call | tf_op jit(solution)/shard_map/exchange_and_grads/pallas_call | solution.py:530
  40.5 4.5 %write_and_reduce.1 = (bf16[16,8,2560]{2,1,0:T(8,128)(2,1)}, bf16[16,8,2560]{2,1,0:T(8,128)(2,1)}, bf16[16,8,2560]{2,1,0:T(8,128)(2,1)}, f32[2,512]{1,0:T(2,128)...) custom-call(bf16[3,16,8,2560]{3,2,1,0:T(8,128)(2,1)} %get-tuple-element.18.grads_ref, ...), custom_call_target="tpu_custom_call" | custom-call | tf_op jit(solution)/shard_map/write_and_reduce/pallas_call | solution.py:583

commit v2 on v1

--- a/solution.py
+++ b/solution.py
@@ -15,6 +15,7 @@
 ROOM = 9
 SIDE = ROOM * 16
 BOTH = 2 * SIDE
+EARLY = 2
 BF16 = jnp.bfloat16
 F32 = jnp.float32
 HIGHEST = lax.Precision.HIGHEST
@@ -59,6 +60,11 @@
     b = rest.astype(BF16)
     c = (rest - b.astype(F32)).astype(BF16)
     return jnp.concatenate([a, b, c], axis=0)
+
+
+def two_parts(x):
+    a = x.astype(BF16)
+    return a, (x - a.astype(F32)).astype(BF16)
 
 
 def west_heads(shift):
@@ -95,10 +101,22 @@
     offset_hbm,
     second_hbm,
     keybias_hbm,
+    gq_hbm,
+    gk_hbm,
+    gv_hbm,
+    gfirst_ref,
+    goffset_ref,
+    gsecond_ref,
+    gkey_ref,
     out_ref,
     sums_ref,
     seconds_ref,
     layer_ref,
+    hidden_ref,
+    slope_ref,
+    merged_ref,
+    probs_ref,
+    dscores_ref,
     held,
     own,
     packed,
@@ -135,6 +153,7 @@
     z_recv,
     xy_send,
     xy_recv,
+    out_sem,
 ):
     y = lax.axis_index("dp")
     sp = lax.axis_index("space")
@@ -145,12 +164,12 @@
     east_id = {"space": (sp + 1) % 32}
     slow_id = {"space": (sp + 31 + 2 * core) % 32}
     near = []
-    for k in range(1, 16):
+    for k in sorted(range(1, 16), key=lambda k: -(k // 8 + 2 - abs((k // 2) % 4 - 2))):
         xx, yy, cc = (x_lo + k // 8) % 2, (y + (k // 2) % 4) % 4, (core + k) % 2
         near.append((xx * 4 + yy, {"dp": yy, "space": xx * 16 + z * 2 + cc}))
-    z_ids = [{"space": x_lo * 16 + ((z + k) % 8) * 2 + core} for k in range(1, 8)]
+    z_ids = [{"space": x_lo * 16 + ((z + k) % 8) * 2 + core} for k in (4, 3, 5, 2, 6, 1, 7)]
     xy_ids = []
-    for k in range(1, 16):
+    for k in sorted(range(1, 16), key=lambda k: -(4 - abs(k // 4 - 2) - abs(k % 4 - 2))):
         xx, yy = (x + k // 4) % 4, (y + k % 4) % 4
         xy_ids.append({"dp": yy, "space": (xx % 2) * 16 + z * 2 + core, "tensor": xx // 2})
     other_ids = []
@@ -158,6 +177,11 @@
         xx, yy = (x_lo + k // 4) % 2, (y + k % 4) % 4
         other_ids.append({"dp": yy, "space": xx * 16 + z * 2 + core, "tensor": 1 - t})
     tensor_id = {"tensor": 1 - t}
+
+    greeted = z_ids + other_ids + [to for _, to in near] + [slow_id]
+    barrier = pltpu.get_barrier_semaphore()
+    for to in greeted:
+        pl.semaphore_signal(barrier, inc=1, device_id=to, device_id_type=MESH)
 
     fields = (q_ref, k_ref, v_ref, d_ref)
     small = [
@@ -180,10 +204,6 @@
     for copy in small[1:]:
         copy.start()
 
-    barrier = pltpu.get_barrier_semaphore()
-    for to in [slow_id] + [i for _, i in near] + z_ids + other_ids:
-        pl.semaphore_signal(barrier, inc=1, device_id=to, device_id_type=MESH)
-
     def side_rows(side):
         return pl.ds(side * SIDE, SIDE)
 
@@ -235,7 +255,7 @@
     for copy in loads:
         copy.wait()
     pack(0)
-    pl.semaphore_wait(barrier, 31)
+    pl.semaphore_wait(barrier, len(greeted))
     for side in range(2):
         in_copy(side, 0).start()
 
@@ -311,58 +331,78 @@
 
     scale = 128.0 ** -0.5
 
-    @pl.loop(0, CHUNKS)
-    def _(c):
-        front = iota((64, 128), 1) < 64
-
-        def paired(x):
-            return jnp.where(front, x[0:64], x[64:128])
-
-        def split(x):
-            return jnp.concatenate(
-                [jnp.where(front, x, 0.0), jnp.where(front, 0.0, x)], axis=0
-            ).astype(BF16)
-
+    front = iota((64, 128), 1) < 64
+    lane8 = iota((8, 128), 1)
+
+    def paired(x):
+        return jnp.where(front, x[0:64], x[64:128])
+
+    def split(x):
+        return jnp.concatenate([jnp.where(front, x, 0.0), jnp.where(front, 0.0, x)], axis=0)
+
+    def receive(c):
         for side in range(2):
             in_copy(side, c).wait_recv()
+
+    def give_back(c):
+        for side in range(2):
+            back_copy(side, c).start()
+
+    def attention(c):
         theirs = lent[c]
         merged = []
         for i in range(GROUP):
             both = jnp.concatenate([own[c, 128 * i : 128 * i + 128, :], theirs], axis=0)
             whole = dot(merge[i], both, 1, 0).astype(BF16)
+            merged_ref[c % 2, i] = whole
             merged.append([whole[:, 128 * a : 128 * a + 128] for a in range(4)])
         scores = [paired(dot(f[1], f[0], 1, 1)) for f in merged]
         dprobs = [paired(dot(f[2], f[3], 1, 1)) for f in merged]
-        probs, dscores = [], []
         for i in range(GROUP):
-            sc = scores[i] * (scale * LOG2E) + bias[c * GROUP + i]
+            h = c * GROUP + i
+            sc = scores[i] * (scale * LOG2E) + bias[h]
             e = jnp.exp2(sc - jnp.max(sc, axis=0, keepdims=True))
             p = e * (1.0 / jnp.sum(e, axis=0, keepdims=True))
             pd = p * dprobs[i]
-            probs.append(p)
-            dscores.append(pd - p * jnp.sum(pd, axis=0, keepdims=True))
-        lane8 = iota((8, 128), 1)
-        for i in range(GROUP):
+            ds = pd - p * jnp.sum(pd, axis=0, keepdims=True)
+            probs_ref[c % 2, i] = split(p).astype(BF16)
+            dscores_ref[c % 2, i] = split(ds).astype(BF16)
             acc = jnp.zeros((8, 128), F32)
             land_acc = jnp.zeros((8, 128), F32)
             for rj in range(8):
                 at = slice(8 * rj, 8 * rj + 8)
-                part = dscores[i][at]
+                part = ds[at]
                 land_acc += part * is_land[i, at]
                 both = jnp.where(lane8 < 64, part + pltpu.roll(part, 64, 1), 0.0)
                 acc += pltpu.roll(both, 128 - 8 * rj, 1) if rj else both
-            at = pl.ds(pl.multiple_of((c * GROUP + i) * 8, 8), 8)
+            at = pl.ds(pl.multiple_of(h * 8, 8), 8)
             rows[at, :] = acc
             land_rows[at, :] = land_acc
+
+    def gradients(c):
         for i in range(GROUP):
-            f, at = merged[i], slice(128 * i, 128 * i + 128)
-            p_low, ds_low = split(probs[i]), split(dscores[i])
-            window[c, at, 0:128] = (dot(ds_low, f[1], 0, 0) * scale).astype(BF16)
-            window[c, at, 128:256] = (dot(ds_low, f[0], 1, 0) * scale).astype(BF16)
-            window[c, at, 256:384] = dot(p_low, f[3], 1, 0).astype(BF16)
+            f, at = merged_ref[c % 2, i], slice(128 * i, 128 * i + 128)
+            p_low, ds_low = probs_ref[c % 2, i], dscores_ref[c % 2, i]
+            window[c, at, 0:128] = (dot(ds_low, f[:, 128:256], 0, 0) * scale).astype(BF16)
+            window[c, at, 128:256] = (dot(ds_low, f[:, 0:128], 1, 0) * scale).astype(BF16)
+            window[c, at, 256:384] = dot(p_low, f[:, 384:512], 1, 0).astype(BF16)
         far[c] = dot(pack_back[...], window[c], 1, 0).astype(BF16)
-        for side in range(2):
-            back_copy(side, c).start()
+
+    receive(0)
+    attention(0)
+
+    @pl.loop(1, CHUNKS - 1)
+    def _(c):
+        receive(c)
+        attention(c)
+        gradients(c - 1)
+
+        @pl.when(c <= EARLY)
+        def _():
+            give_back(c - 1)
+
+    receive(CHUNKS - 1)
+    attention(CHUNKS - 1)
 
     pad = jnp.zeros((4, 1024), F32)
     flat = jnp.concatenate([rows[pl.ds(cj, HEADS, stride=8), :] for cj in range(8)], axis=1)
@@ -390,6 +430,13 @@
             for i, (src, dst, send, recv, to) in enumerate(pieces)
         ]
 
+    def out_copies(c):
+        lanes = pl.ds(pl.multiple_of(c * LANES, LANES), LANES)
+        return [
+            pltpu.make_async_copy(out_ref.at[a, :, :, lanes], out.at[:, :, lanes], out_sem.at[a, c])
+            for a, out in enumerate((gq_hbm, gk_hbm, gv_hbm))
+        ]
+
     def finish(c):
         for side in range(2):
             back_copy(side, c).wait_recv()
@@ -400,6 +447,8 @@
             whole = dot(place[i], both, 1, 0).astype(BF16)
             for a in range(3):
                 out_ref[a, :, :, lanes] = whole[:, 128 * a : 128 * a + 128].reshape(16, 8, 128)
+        for copy in out_copies(c):
+            copy.start()
 
     slot = x_lo * 4 + y
     copies = exchange(
@@ -408,8 +457,15 @@
     for copy in copies:
         copy.start()
     near_part[slot * 2 + core] = table_part[slot]
+    gradients(CHUNKS - 2)
+    gradients(CHUNKS - 1)
+    second_copy.wait()
+    pre, cy, cx = hidden_before(layer_ref[0:2, :], layer_ref[2:3, :])
+    hidden = jnp.maximum(pre, 0.0)
+    hidden_ref[0], hidden_ref[1] = two_parts(hidden)
+    sent = copies
     for copy in copies:
-        copy.wait()
+        copy.wait_recv()
     mine = near_part[0]
     for i in range(1, 16):
         mine = mine + near_part[i]
@@ -419,12 +475,19 @@
     for copy in copies:
         copy.start()
 
+    for c in range(EARLY, CHUNKS):
+        give_back(c)
+    for half in range(2):
+        p = jax.nn.sigmoid(dot(seconds_ref[half], hidden, 1, 1, HIGHEST))
+        slope_ref[half] = jnp.where(used_bins(HEADS), 16.0 * p * (1.0 - p), 0.0)
+
     @pl.loop(0, 2)
     def _(c):
         finish(c)
 
+    sent = sent + copies
     for copy in copies:
-        copy.wait()
+        copy.wait_recv()
     mine = z_part[0]
     for i in range(1, 8):
         mine = mine + z_part[i]
@@ -439,57 +502,18 @@
     def _(c):
         finish(c)
 
-    second_copy.wait()
-
     @pl.loop(0, CHUNKS)
     def _(c):
         for side in range(2):
             in_copy(side, c).wait_send()
             back_copy(side, c).wait_send()
 
+    seconds = jnp.concatenate([seconds_ref[0], seconds_ref[1]], axis=0)
+    seconds_high, seconds_low = two_parts(seconds)
+    seconds_three = jnp.concatenate([seconds_high, seconds_high, seconds_low], axis=0)
+    sent = sent + copies
     for copy in copies:
-        copy.wait()
-
-
-def last_kernel(
-    grads_ref,
-    sums_hbm,
-    seconds_hbm,
-    layer_hbm,
-    gq_ref,
-    gk_ref,
-    gv_ref,
-    gfirst_ref,
-    goffset_ref,
-    gsecond_ref,
-    gkey_ref,
-    sums_ref,
-    seconds_ref,
-    layer_ref,
-    held,
-    sem,
-):
-    small = [
-        pltpu.make_async_copy(a, b, sem.at[3 + i])
-        for i, (a, b) in enumerate(
-            ((layer_hbm, layer_ref), (seconds_hbm, seconds_ref), (sums_hbm, sums_ref))
-        )
-    ]
-    for copy in small:
-        copy.start()
-    outs = (gq_ref, gk_ref, gv_ref)
-    loads = [pltpu.make_async_copy(grads_ref.at[a], held.at[a], sem.at[6 + a]) for a in range(3)]
-    copies = [pltpu.make_async_copy(held.at[a], outs[a], sem.at[a]) for a in range(3)]
-    for copy in loads:
-        copy.start()
-    for copy in small:
-        copy.wait()
-    for load, copy in zip(loads, copies):
-        load.wait()
-        copy.start()
-    t = lax.axis_index("tensor")
-    pre, cy, cx = hidden_before(layer_ref[0:2, :], layer_ref[2:3, :])
-    hidden = jnp.maximum(pre, 0.0)
+        copy.wait_recv()
 
     def bins(half):
         strips = [
@@ -498,15 +522,14 @@
         ]
         return jnp.concatenate(strips, axis=0)
 
-    def pulled(half):
-        logits = dot(seconds_ref[half], hidden, 1, 1, HIGHEST)
-        p = jax.nn.sigmoid(logits)
-        return jnp.where(used_bins(HEADS), bins(half)[0:HEADS] * (16.0 * p * (1.0 - p)), 0.0)
-
-    low, high = pulled(0), pulled(1)
-    mine = jnp.where(t == 0, low, high)
-    gsecond_ref[...] = dot(mine, hidden, 1, 0, HIGHEST)
-    ghidden = dot(low, seconds_ref[0], 0, 0, HIGHEST) + dot(high, seconds_ref[1], 0, 0, HIGHEST)
+    pulled = [bins(half)[0:HEADS] * slope_ref[half] for half in range(2)]
+    high, low = two_parts(jnp.where(t == 0, pulled[0], pulled[1]))
+    gsecond = dot(jnp.concatenate([high, low], axis=0), hidden_ref[0], 1, 0)
+    gsecond_ref[...] = (
+        gsecond[0:HEADS] + gsecond[HEADS : 2 * HEADS] + dot(high, hidden_ref[1], 1, 0)
+    )
+    high, low = two_parts(jnp.concatenate(pulled, axis=0))
+    ghidden = dot(jnp.concatenate([high, low, high], axis=0), seconds_three, 0, 0)
     ghidden = jnp.where(pre > 0.0, ghidden, 0.0)
     gfirst_ref[0:1, :] = jnp.sum(cy * ghidden, axis=0, keepdims=True)
     gfirst_ref[1:2, :] = jnp.sum(cx * ghidden, axis=0, keepdims=True)
@@ -515,6 +538,30 @@
     pick = jnp.where(n == 24, jnp.where(r == 0, -1.0, 1.0), jnp.where((n == 8) & (r == 0), 1.0, 0.0))
     keys = dot(pick, jnp.where(t == 0, bins(0), bins(1)), 1, 1, HIGHEST)
     gkey_ref[...] = keys[0:2, 0:HEADS]
+    for copy in sent:
+        copy.wait_send()
+
+    @pl.loop(0, CHUNKS)
+    def _(c):
+        for copy in out_copies(c):
+            copy.wait()
+
+
+def last_kernel(*refs):
+    n = len(refs) // 3
+    given, placed, held, sem = refs[:n], refs[n : 2 * n], refs[2 * n : 3 * n], refs[3 * n]
+    pieces = [(i, pl.ds(4 * part, 4)) for part in range(4) for i in range(3)]
+    pieces += [(i, slice(None)) for i in range(3, n)]
+    loads, copies = [], []
+    for at, (i, part) in enumerate(pieces):
+        here = held[i].at[part]
+        loads.append(pltpu.make_async_copy(given[i].at[part], here, sem.at[0, at]))
+        copies.append(pltpu.make_async_copy(here, placed[i].at[part], sem.at[1, at]))
+    for load in loads:
+        load.start()
+    for load, copy in zip(loads, copies):
+        load.wait()
+        copy.start()
     for copy in copies:
         copy.wait()
 
@@ -527,17 +574,27 @@
     hbm = pl.BlockSpec(memory_space=pltpu.HBM)
     dma = pltpu.SemaphoreType.DMA
     vec = pltpu.VMEM
+    results = (jax.ShapeDtypeStruct(field, BF16),) * 3 + (
+        jax.ShapeDtypeStruct((2, 512), F32),
+        jax.ShapeDtypeStruct((1, 512), F32),
+        jax.ShapeDtypeStruct((HEADS, 512), F32),
+        jax.ShapeDtypeStruct((2, HEADS), F32),
+    )
     outs = pl.pallas_call(
         main_kernel,
-        out_shape=(
-            jax.ShapeDtypeStruct((3,) + field, BF16),
-            jax.ShapeDtypeStruct((16, 8, 128), F32),
-            jax.ShapeDtypeStruct((2, HEADS, 512), F32),
-            jax.ShapeDtypeStruct((3, 512), F32),
-        ),
+        out_shape=results,
         in_specs=[hbm] * 10,
-        out_specs=(vmem,) * 4,
+        out_specs=(hbm,) * 3 + (vmem,) * 4,
         scratch_shapes=[
+            vec((3,) + field, BF16),
+            vec((16, 8, 128), F32),
+            vec((2, HEADS, 512), F32),
+            vec((3, 512), F32),
+            vec((2, 256, 512), BF16),
+            vec((2, HEADS, 256), F32),
+            vec((2, GROUP, 128, 512), BF16),
+            vec((2, GROUP, 128, 128), BF16),
+            vec((2, GROUP, 128, 128), BF16),
             vec((4,) + field, BF16),
             vec((CHUNKS, GROUP * 128, 512), BF16),
             vec((CHUNKS, BOTH, 512), BF16),
@@ -574,6 +631,7 @@
             dma((7,)),
             dma((15,)),
             dma((15,)),
+            dma((3, CHUNKS)),
         ],
         compiler_params=pltpu.CompilerParams(
             collective_id=0, has_side_effects=True, vmem_limit_bytes=60 * 2**20
@@ -582,22 +640,10 @@
     )(*fields, land, shifts, first, offset.reshape(1, 512), second.T, keybias)
     gq, gk, gv, gfirst, goffset, gsecond, gkey = pl.pallas_call(
         last_kernel,
-        out_shape=(jax.ShapeDtypeStruct(field, BF16),) * 3
-        + (
-            jax.ShapeDtypeStruct((2, 512), F32),
-            jax.ShapeDtypeStruct((1, 512), F32),
-            jax.ShapeDtypeStruct((HEADS, 512), F32),
-            jax.ShapeDtypeStruct((2, HEADS), F32),
-        ),
-        in_specs=[hbm] * 4,
-        out_specs=(hbm,) * 3 + (vmem,) * 4,
-        scratch_shapes=[
-            vec((16, 8, 128), F32),
-            vec((2, HEADS, 512), F32),
-            vec((3, 512), F32),
-            vec((3,) + field, BF16),
-            dma((9,)),
-        ],
+        out_shape=results,
+        in_specs=[hbm] * 7,
+        out_specs=(hbm,) * 7,
+        scratch_shapes=[vec(r.shape, r.dtype) for r in results] + [dma((2, 16))],
         compiler_params=pltpu.CompilerParams(vmem_limit_bytes=60 * 2**20),
         name="write_and_reduce",
     )(*outs)

time: 45.4 us -> 41.9 us (0.923)
  Pallas kernels: 44.4 us -> 41.1 us
    pallas_call x2, Pallas kernels: 44.4 us -> 41.1 us  [the longest x1 38.5 us: on_device(): pl.pallas_call(main_kernel, out_shape=results, in_specs=[hbm] * 10, out_s...]
where the time goes in v2:
time: 41.9 us; the launch traced here: 41.7 us
  Pallas kernels  41.1 us (98%)
  between operations  0.64 us (2%)
    pallas_call x1, Pallas kernels, on_device(): pl.pallas_call(main_kernel, out_shape=results, in_specs=[hbm] * 10, out_s...  38.5 us
    pallas_call x1, Pallas kernels, on_device(): pl.pallas_call(last_kernel, out_shape=results, in_specs=[hbm] * 7, out_sp...  2.58 us

profile of v2, /device:TPU:1, one launch (start us, length us, event | category | flops | bytes accessed | tf_op | source)
XLA Modules:
  0.0 41.7 jit_solution(9708294420860918922)
XLA Ops:
  0.6 38.5 %exchange_and_grads.1 = (bf16[16,8,2560]{2,1,0:T(8,128)(2,1)}, bf16[16,8,2560]{2,1,0:T(8,128)(2,1)}, bf16[16,8,2560]{2,1,0:T(8,128)(2,1)}, f32[2,512]{1,0:T(2,12...) custom-call(bf16[16,8,2560]{2,1,0:T(8,128)(2,1)} %bitcast.11, bf16[16,8,2560]{2,1,0:T(8,128)(2,1)} %bitcast.12, ...), custom_call_target="tpu_custom_call" | custom-call | tf_op jit(solution)/shard_map/exchange_and_grads/pallas_call | solution.py:583
  39.2 2.6 %write_and_reduce.1 = (bf16[16,8,2560]{2,1,0:T(8,128)(2,1)}, bf16[16,8,2560]{2,1,0:T(8,128)(2,1)}, bf16[16,8,2560]{2,1,0:T(8,128)(2,1)}, f32[2,512]{1,0:T(2,128)...) custom-call(bf16[16,8,2560]{2,1,0:T(8,128)(2,1)} %get-tuple-element.21.refs_0_, ...), custom_call_target="tpu_custom_call" | custom-call | tf_op jit(solution)/shard_map/write_and_reduce/pallas_call | solution.py:641

commit v3 on v2

--- a/solution.py
+++ b/solution.py
@@ -15,7 +15,7 @@
 ROOM = 9
 SIDE = ROOM * 16
 BOTH = 2 * SIDE
-EARLY = 2
+EARLY = 3
 BF16 = jnp.bfloat16
 F32 = jnp.float32
 HIGHEST = lax.Precision.HIGHEST
@@ -154,6 +154,7 @@
     xy_send,
     xy_recv,
     out_sem,
+    round_sem,
 ):
     y = lax.axis_index("dp")
     sp = lax.axis_index("space")
@@ -177,11 +178,7 @@
         xx, yy = (x_lo + k // 4) % 2, (y + k % 4) % 4
         other_ids.append({"dp": yy, "space": xx * 16 + z * 2 + core, "tensor": 1 - t})
     tensor_id = {"tensor": 1 - t}
-
-    greeted = z_ids + other_ids + [to for _, to in near] + [slow_id]
-    barrier = pltpu.get_barrier_semaphore()
-    for to in greeted:
-        pl.semaphore_signal(barrier, inc=1, device_id=to, device_id_type=MESH)
+    core_id = {"space": sp + 1 - 2 * core}
 
     fields = (q_ref, k_ref, v_ref, d_ref)
     small = [
@@ -204,6 +201,25 @@
     for copy in small[1:]:
         copy.start()
 
+    steps = [slow_id, core_id]
+    steps += [{"space": x_lo * 16 + ((z + k) % 8) * 2 + core} for k in (1, 7)]
+    steps += [{"dp": (y + k) % 4} for k in (1, 3)]
+    for k in (1, 3):
+        xx = (x + k) % 4
+        steps.append({"space": (xx % 2) * 16 + z * 2 + core, "tensor": xx // 2})
+    barrier = pltpu.get_barrier_semaphore()
+    for to in steps:
+        pl.semaphore_signal(barrier, inc=1, device_id=to, device_id_type=MESH)
+
+    def tell(round_at):
+        for to in steps:
+            pl.semaphore_signal(
+                round_sem.at[round_at], inc=1, device_id=to, device_id_type=MESH
+            )
+
+    def hear(round_at):
+        pl.semaphore_wait(round_sem.at[round_at], len(steps))
+
     def side_rows(side):
         return pl.ds(side * SIDE, SIDE)
 
@@ -255,9 +271,10 @@
     for copy in loads:
         copy.wait()
     pack(0)
-    pl.semaphore_wait(barrier, len(greeted))
+    pl.semaphore_wait(barrier, len(steps))
     for side in range(2):
         in_copy(side, 0).start()
+    tell(0)
 
     @pl.loop(1, CHUNKS)
     def _(c):
@@ -265,7 +282,6 @@
         for side in range(2):
             in_copy(side, c).start()
 
-    second_copy.start()
     for copy in small[1:]:
         copy.wait()
     seconds_ref[t] = second_ref[...]
@@ -287,12 +303,13 @@
     logits = dot(second_ref[...], jnp.maximum(pre, 0.0), 1, 1, HIGHEST)
     table = jnp.where(used_bins(HEADS), 16.0 * jax.nn.sigmoid(logits), 0.0)
     table = three_parts(jnp.concatenate([table, jnp.zeros((4, 256), F32)], axis=0))
-    b, l = iota((256, 128), 0), iota((256, 128), 1)
     for cj in range(8):
+        b, l = iota((128, 256), 1), iota((128, 256), 0)
         here = (b == (l // 8) * 16 + (l % 8 - cj + 16) % 16) | (b == 8) | (b == 24)
-        sel = onehot(here)
-        expand[:, cj * 128 : (cj + 1) * 128] = sel
-        wide = dot(table, sel, 1, 0)
+        expand[cj * 128 : (cj + 1) * 128, :] = onehot(here)
+        b, l = iota((256, 128), 0), iota((256, 128), 1)
+        here = b == (l // 8) * 16 + (l % 8 - cj + 16) % 16
+        wide = dot(table, onehot(here), 1, 0)
         wide = wide[0:24] + wide[24:48] + wide[48:72]
         rows[pl.ds(cj, HEADS, stride=8), :] = wide[0:HEADS]
 
@@ -329,6 +346,9 @@
                 key = jnp.where(is_land[i, at] > 0.5, high, low) + masked[at]
                 bias[h, at, :] = jnp.where(lane < 64, left, right) * LOG2E + key
 
+    hear(0)
+    tell(1)
+    second_copy.start()
     scale = 128.0 ** -0.5
 
     front = iota((64, 128), 1) < 64
@@ -390,6 +410,8 @@
 
     receive(0)
     attention(0)
+    hear(1)
+    tell(2)
 
     @pl.loop(1, CHUNKS - 1)
     def _(c):
@@ -403,6 +425,7 @@
 
     receive(CHUNKS - 1)
     attention(CHUNKS - 1)
+    hear(2)
 
     pad = jnp.zeros((4, 1024), F32)
     flat = jnp.concatenate([rows[pl.ds(cj, HEADS, stride=8), :] for cj in range(8)], axis=1)
@@ -410,7 +433,7 @@
         [land_rows[pl.ds(cj, HEADS, stride=8), :] for cj in range(8)], axis=1
     )
     stacked = three_parts(jnp.concatenate([flat, pad, land_flat, pad], axis=0))
-    binned = dot(stacked, expand[...], 1, 1)
+    binned = dot(stacked, expand[...], 1, 0)
     binned = binned[0:48] + binned[48:96] + binned[96:144]
     binned = jnp.where(iota((24, 256), 1) == 24, binned[24:48], binned[0:24])
     for i in range(6):
@@ -603,7 +626,7 @@
             vec((CHUNKS, BOTH, 384), BF16),
             vec((CHUNKS, BOTH, 384), BF16),
             vec((HEADS, 64, 128), F32),
-            vec((256, 1024), BF16),
+            vec((1024, 256), BF16),
             vec((HEADS * 8, 128), F32),
             vec((HEADS * 8, 128), F32),
             vec((GROUP, 64, 128), F32),
@@ -632,6 +655,7 @@
             dma((15,)),
             dma((15,)),
             dma((3, CHUNKS)),
+            pltpu.SemaphoreType.REGULAR((3,)),
         ],
         compiler_params=pltpu.CompilerParams(
             collective_id=0, has_side_effects=True, vmem_limit_bytes=60 * 2**20

time: 41.9 us -> 40.3 us (0.962)
  Pallas kernels: 41.1 us -> 39.5 us
    pallas_call x1, Pallas kernels: 38.5 us -> 36.9 us  [on_device(): pl.pallas_call(main_kernel, out_shape=results, in_specs=[hbm] * 10, out_s...]
where the time goes in v3:
time: 40.3 us; the launch traced here: 40.1 us
  Pallas kernels  39.5 us (98%)
  between operations  0.64 us (2%)
    pallas_call x1, Pallas kernels, on_device(): pl.pallas_call(main_kernel, out_shape=results, in_specs=[hbm] * 10, out_s...  36.9 us
    pallas_call x1, Pallas kernels, on_device(): pl.pallas_call(last_kernel, out_shape=results, in_specs=[hbm] * 7, out_sp...  2.58 us

profile of v3, /device:TPU:1, one launch (start us, length us, event | category | flops | bytes accessed | tf_op | source)
XLA Modules:
  0.0 40.1 jit_solution(7604651002274626785)
XLA Ops:
  0.6 36.9 %exchange_and_grads.1 = (bf16[16,8,2560]{2,1,0:T(8,128)(2,1)}, bf16[16,8,2560]{2,1,0:T(8,128)(2,1)}, bf16[16,8,2560]{2,1,0:T(8,128)(2,1)}, f32[2,512]{1,0:T(2,12...) custom-call(bf16[16,8,2560]{2,1,0:T(8,128)(2,1)} %bitcast.11, bf16[16,8,2560]{2,1,0:T(8,128)(2,1)} %bitcast.12, ...), custom_call_target="tpu_custom_call" | custom-call | tf_op jit(solution)/shard_map/exchange_and_grads/pallas_call | solution.py:606
  37.6 2.6 %write_and_reduce.1 = (bf16[16,8,2560]{2,1,0:T(8,128)(2,1)}, bf16[16,8,2560]{2,1,0:T(8,128)(2,1)}, bf16[16,8,2560]{2,1,0:T(8,128)(2,1)}, f32[2,512]{1,0:T(2,128)...) custom-call(bf16[16,8,2560]{2,1,0:T(8,128)(2,1)} %get-tuple-element.21.refs_0_, ...), custom_call_target="tpu_custom_call" | custom-call | tf_op jit(solution)/shard_map/write_and_reduce/pallas_call | solution.py:665

commit v4 on v3

--- a/solution.py
+++ b/solution.py
@@ -15,7 +15,7 @@
 ROOM = 9
 SIDE = ROOM * 16
 BOTH = 2 * SIDE
-EARLY = 3
+EARLY = 2
 BF16 = jnp.bfloat16
 F32 = jnp.float32
 HIGHEST = lax.Precision.HIGHEST
@@ -194,11 +194,18 @@
             )
         )
     ]
-    loads = [pltpu.make_async_copy(ref, held.at[a], load_sem.at[a]) for a, ref in enumerate(fields)]
+    loads = []
+    for part, lanes in enumerate((pl.ds(0, LANES), pl.ds(LANES, (CHUNKS - 1) * LANES))):
+        loads.append(
+            [
+                pltpu.make_async_copy(
+                    ref.at[:, :, lanes], held.at[a, :, :, lanes], load_sem.at[part, a]
+                )
+                for a, ref in enumerate(fields)
+            ]
+        )
     small[0].start()
-    for copy in loads:
-        copy.start()
-    for copy in small[1:]:
+    for copy in loads[0]:
         copy.start()
 
     steps = [slow_id, core_id]
@@ -211,6 +218,9 @@
     for to in steps:
         pl.semaphore_signal(barrier, inc=1, device_id=to, device_id_type=MESH)
 
+    for copy in loads[1] + small[1:]:
+        copy.start()
+
     def tell(round_at):
         for to in steps:
             pl.semaphore_signal(
@@ -268,13 +278,15 @@
                 ].reshape(128, 128)
         packed[c] = dot(pack_in[...], own[c], 1, 0).astype(BF16)
 
-    for copy in loads:
+    for copy in loads[0]:
         copy.wait()
     pack(0)
     pl.semaphore_wait(barrier, len(steps))
     for side in range(2):
         in_copy(side, 0).start()
     tell(0)
+    for copy in loads[1]:
+        copy.wait()
 
     @pl.loop(1, CHUNKS)
     def _(c):
@@ -482,6 +494,8 @@
     near_part[slot * 2 + core] = table_part[slot]
     gradients(CHUNKS - 2)
     gradients(CHUNKS - 1)
+    for c in range(EARLY, CHUNKS):
+        give_back(c)
     second_copy.wait()
     pre, cy, cx = hidden_before(layer_ref[0:2, :], layer_ref[2:3, :])
     hidden = jnp.maximum(pre, 0.0)
@@ -498,8 +512,6 @@
     for copy in copies:
         copy.start()
 
-    for c in range(EARLY, CHUNKS):
-        give_back(c)
     for half in range(2):
         p = jax.nn.sigmoid(dot(seconds_ref[half], hidden, 1, 1, HIGHEST))
         slope_ref[half] = jnp.where(used_bins(HEADS), 16.0 * p * (1.0 - p), 0.0)
@@ -641,7 +653,7 @@
             vec((HEADS, 512), F32),
             pltpu.SMEM((2,), jnp.int32),
             pltpu.SMEM((2, HEADS), F32),
-            dma((4,)),
+            dma((2, 4)),
             dma((6,)),
             dma((2, CHUNKS)),
             dma((2, CHUNKS)),

time: 40.3 us -> 40.3 us (level)
  no operation moved by 1% of the time
where the time goes in v4:
time: 40.3 us; the launch traced here: 40.1 us
  Pallas kernels  39.5 us (98%)
  between operations  0.64 us (2%)
    pallas_call x1, Pallas kernels, on_device(): pl.pallas_call(main_kernel, out_shape=results, in_specs=[hbm] * 10, out_s...  36.9 us
    pallas_call x1, Pallas kernels, on_device(): pl.pallas_call(last_kernel, out_shape=results, in_specs=[hbm] * 7, out_sp...  2.58 us

profile of v4, /device:TPU:1, one launch (start us, length us, event | category | flops | bytes accessed | tf_op | source)
XLA Modules:
  0.0 40.1 jit_solution(5113109630643505284)
XLA Ops:
  0.6 36.9 %exchange_and_grads.1 = (bf16[16,8,2560]{2,1,0:T(8,128)(2,1)}, bf16[16,8,2560]{2,1,0:T(8,128)(2,1)}, bf16[16,8,2560]{2,1,0:T(8,128)(2,1)}, f32[2,512]{1,0:T(2,12...) custom-call(bf16[16,8,2560]{2,1,0:T(8,128)(2,1)} %bitcast.11, bf16[16,8,2560]{2,1,0:T(8,128)(2,1)} %bitcast.12, ...), custom_call_target="tpu_custom_call" | custom-call | tf_op jit(solution)/shard_map/exchange_and_grads/pallas_call | solution.py:618
  37.5 2.6 %write_and_reduce.1 = (bf16[16,8,2560]{2,1,0:T(8,128)(2,1)}, bf16[16,8,2560]{2,1,0:T(8,128)(2,1)}, bf16[16,8,2560]{2,1,0:T(8,128)(2,1)}, f32[2,512]{1,0:T(2,128)...) custom-call(bf16[16,8,2560]{2,1,0:T(8,128)(2,1)} %get-tuple-element.21.refs_0_, ...), custom_call_target="tpu_custom_call" | custom-call | tf_op jit(solution)/shard_map/write_and_reduce/pallas_call | solution.py:677
